TPU v7x, 256 devices: a whole 4x4x8 slice. The times are simulated.
256 devices in a mesh: orient: 64 (over x, y_hi, z), dom: 4 (over y_lo, core).
Axes of the slice: x: 4, y: 4 (y_hi: 2, y_lo: 2; y = y_hi * 2 + y_lo), z: 8, core: 2. Of those that a mesh axis runs over, the one named last changes fastest.
Arguments:
- images: bfloat16 [256, 2, 4096], P(('orient', 'dom')), may hold values from -6 to 6
- offsets: int32 [256, 9, 2], P(('orient', 'dom')), may hold values from -5 to 5, as said below
- groups: int32 [256], P(('orient', 'dom')), may hold values from 0 to 7
- defocus: int32 [256], P(('orient', 'dom')), may hold values from 0 to 63
- refs: bfloat16 [8192, 2, 4096], P('orient'), may hold values from -2 to 2
- log_prior: float32 [8192], P('orient'), may hold values from -4 to 4
- noise_inv: float32 [8, 4096], replicated, may hold values from 0.030029297 to 0.12011719
- ctf_table: float32 [64, 4096], replicated, may hold values from 0.05 to 1
Outputs:
- data_sum: float32 [8192, 2, 4096], P('orient', None, 'dom')
- weight_sum: float32 [8192, 4096], P('orient', 'dom')
- evidence: float32 [256], P(('orient', 'dom'))
Inputs may be any that keep to these rules, and one draw needn't show every extreme that they name: offsets[i, t] = centre[i] + (2 (t mod 3) - 2, 2 (t // 3) - 2) for one centre of each particle.
All inputs are finite; a program needn't handle non-finite values.
Results may differ from a plain program's by a relative error of at most 0.025.
Values may be sent and summed in bfloat16 or wider, within the bound.
No kernel may reach another device: no remote copies, remote signals or barrier semaphores. Data moves between devices by JAX's collectives and lax.ppermute only.
A program may use at most 64 MiB of HBM per device.

v0:
```python
import math
import jax
import jax.numpy as jnp
from jax import lax
from jax.sharding import PartitionSpec as P

SIDE = 64
TWO_PI = 2.0 * math.pi
TRANS_VAR = 8.0
CONTRACT_ROWS = (((0,), (0,)), ((), ()))
CONTRACT_LAST = (((1,), (1,)), ((), ()))


def frequencies(count):
    pixel = jnp.arange(count, dtype=jnp.int32)
    half = SIDE // 2
    return ((pixel % SIDE + half) % SIDE - half, (pixel // SIDE + half) % SIDE - half)


def shifted(weighted, shift_x, shift_y, freq_x, freq_y):
    turns = (shift_x[:, None] * freq_x[None, :] + shift_y[:, None] * freq_y[None, :]) % SIDE
    angle = turns.astype(jnp.float32) * (TWO_PI / SIDE)
    cosine = jnp.cos(angle)
    sine = jnp.sin(angle)
    real_part = weighted[:, 0].astype(jnp.float32)
    imag_part = weighted[:, 1].astype(jnp.float32)
    new_real = real_part * cosine + imag_part * sine
    new_imag = imag_part * cosine - real_part * sine
    return jnp.concatenate([new_real, new_imag], axis=1).astype(jnp.bfloat16)


def lookup(index, table):
    picks = (index[:, None] == jnp.arange(table.shape[0], dtype=jnp.int32)[None, :]).astype(
        jnp.float32
    )
    return jnp.dot(picks, table, precision=lax.Precision.HIGHEST)


def on_device(images, offsets, groups, defocus, refs, log_prior, noise_inv, ctf_table):
    own = images.shape[0]
    pixels = images.shape[2]
    count_refs = refs.shape[0]
    trans = offsets.shape[1]
    scale = (
        25.0
        * (count_refs * lax.axis_size("orient"))
        / (own * lax.axis_size("orient") * lax.axis_size("dom"))
    )
    meta = jnp.concatenate(
        [offsets.reshape(own, 2 * trans), groups[:, None], defocus[:, None]], axis=1
    ).astype(jnp.bfloat16)
    gathered, meta_all = (
        lax.all_gather(images, "orient", axis=0, tiled=True),
        lax.all_gather(meta, "orient", axis=0, tiled=True),
    )
    codes = meta_all.astype(jnp.int32)
    shift_x = codes[:, 0 : 2 * trans : 2]
    shift_y = codes[:, 1 : 2 * trans : 2]
    noise_row = lookup(codes[:, 2 * trans], noise_inv)
    ctf_row = lookup(codes[:, 2 * trans + 1], ctf_table)
    product = noise_row * ctf_row
    weighted = (gathered.astype(jnp.float32) * product[:, None, :]).astype(jnp.bfloat16)
    ctf_power = (product * ctf_row).astype(jnp.bfloat16)
    ref_flat = refs.reshape(count_refs, 2 * pixels)
    real_ref = refs[:, 0].astype(jnp.float32)
    imag_ref = refs[:, 1].astype(jnp.float32)
    power = (real_ref * real_ref + imag_ref * imag_ref).astype(jnp.bfloat16)
    self_term = lax.dot_general(ctf_power, power, CONTRACT_LAST, preferred_element_type=jnp.float32)
    freq_x, freq_y = frequencies(pixels)
    crosses = []
    moved_list = []
    for step in range(trans):
        moved = shifted(weighted, shift_x[:, step], shift_y[:, step], freq_x, freq_y)
        moved_list.append(moved)
        crosses.append(
            lax.dot_general(moved, ref_flat, CONTRACT_LAST, preferred_element_type=jnp.float32)
        )
    cross = jnp.stack(crosses)
    prior = -((shift_x * shift_x + shift_y * shift_y).astype(jnp.float32) / (2.0 * TRANS_VAR))
    score = cross - 0.5 * self_term[None, :, :] + prior.T[:, :, None] + log_prior[None, None, :]
    local_top = jnp.max(score, axis=(0, 2))
    top = lax.pmax(local_top, "orient")
    mass = lax.psum(jnp.sum(jnp.exp(score - top[None, :, None]), axis=(0, 2)), "orient")
    evidence = top + jnp.log(mass)
    post = jnp.exp(score - evidence[None, :, None]).astype(jnp.bfloat16)
    post_sum = jnp.sum(post.astype(jnp.float32), axis=0).astype(jnp.bfloat16)
    data_acc = jnp.zeros((count_refs, 2 * pixels), jnp.float32)
    for step in range(trans):
        data_acc = data_acc + lax.dot_general(
            post[step], moved_list[step], CONTRACT_ROWS, preferred_element_type=jnp.float32
        )
    weight_acc = lax.dot_general(
        post_sum, ctf_power, CONTRACT_ROWS, preferred_element_type=jnp.float32
    )
    stacked = (
        jnp.concatenate([data_acc.reshape(count_refs, 2, pixels), weight_acc[:, None, :]], axis=1)
        * scale
    )
    shares = lax.psum_scatter(
        stacked.astype(jnp.bfloat16), "dom", scatter_dimension=2, tiled=True
    ).astype(jnp.float32)
    data_sum = shares[:, 0:2]
    weight_sum = shares[:, 2]
    own_evidence = lax.dynamic_slice_in_dim(evidence, lax.axis_index("orient") * own, own, 0)
    return (data_sum, weight_sum, own_evidence)


def solution(mesh):
    placed = (
        P(("orient", "dom"), None, None),
        P(("orient", "dom"), None, None),
        P(("orient", "dom")),
        P(("orient", "dom")),
        P("orient", None, None),
        P("orient"),
        P(),
        P(),
    )
    return jax.shard_map(
        on_device,
        mesh=mesh,
        in_specs=placed,
        out_specs=(P("orient", None, "dom"), P("orient", "dom"), P(("orient", "dom"))),
        check_vma=False,
    )
```

profile of v0, /device:TPU:1, one launch (start us, length us, event | category | flops | bytes accessed | tf_op | source)
XLA Modules:
  0.0 670.9 jit_solution(16551002698185999900)
XLA Ops:
  7.2 0.7 all-gather.3.cloned.1.call-update
  8.0 0.7 convert.69
  8.6 0.1 copy.31
  10.2 156.5 %all-gather = bf16[64,1,20]{2,1,0:T(2,128)(2,1)S(1)} all-gather(bf16[1,1,20]{2,1,0:T(2,128)(2,1)S(1)} %maximum_bitcast_fusion), channel_id=1, replica_groups=mesh['orient'=64,'dom'=4] {'orient'}, dimensions={0}, use_global_device_ids=true | all-gather | bytes 2600 | tf_op jit(solution)/shard_map/all_gather | solution.py:54
  166.8 0.1 copy.32
  166.9 4.3 copy.40
  171.2 0.6 fusion.97
  171.9 0.2 copy-done.37
  172.1 0.6 multiply_convert_fusion.1
  172.7 0.1 copy-done.2
  172.9 5.1 fusion.130
  178.0 2.4 convolution_multiply_fusion.1
  180.4 2.0 multiply_convert_fusion
  182.4 4.7 fusion.40
  187.1 0.9 fusion.9
  188.0 9.0 %fusion.72 = (bf16[64,4096]{1,0:T(8,128)(2,1)S(1)}, bf16[64,4096]{1,0:T(8,128)(2,1)S(1)}, bf16[64,4096]{1,0:T(8,128)(2,1)S(1)}, bf16[64,4096]{1,0:T(8,128)(2,1)S(1)}) fusion(s32[4096]{0:T(1024)S(1)} %get-tuple-element.68, s32[64]{0:T(128)S(1)} %get-tuple-element.56, s32[4096]{0:T(1024)S(1)} %get-tuple-element.67, s32[64]{0:T(128)S(1)} %get-tuple-element.77, ...), kind=kLoop, calls=%fused_computation.158 | loop fusion | flops 13107200 | bytes 3179520 | tf_op jit(solution)/shard_map/convert.3
  197.1 0.8 fusion.8
  197.9 9.6 %fusion.68 = (bf16[64,4096]{1,0:T(8,128)(2,1)S(1)}, bf16[64,4096]{1,0:T(8,128)(2,1)S(1)}, bf16[64,4096]{1,0:T(8,128)(2,1)S(1)}, bf16[64,4096]{1,0:T(8,128)(2,1)S(1)}) fusion(s32[4096]{0:T(1024)S(1)} %get-tuple-element.68, s32[64]{0:T(128)S(1)} %get-tuple-element.57, s32[4096]{0:T(1024)S(1)} %get-tuple-element.67, s32[64]{0:T(128)S(1)} %get-tuple-element.76, ...), kind=kLoop, calls=%fused_computation.154 | loop fusion | flops 13107200 | bytes 3179520 | tf_op jit(solution)/shard_map/convert.5
  207.6 0.8 fusion.7
  208.4 9.0 %fusion.64 = (bf16[64,4096]{1,0:T(8,128)(2,1)S(1)}, bf16[64,4096]{1,0:T(8,128)(2,1)S(1)}, bf16[64,4096]{1,0:T(8,128)(2,1)S(1)}, bf16[64,4096]{1,0:T(8,128)(2,1)S(1)}) fusion(s32[4096]{0:T(1024)S(1)} %get-tuple-element.68, s32[64]{0:T(128)S(1)} %get-tuple-element.58, s32[4096]{0:T(1024)S(1)} %get-tuple-element.67, s32[64]{0:T(128)S(1)} %get-tuple-element.75, ...), kind=kLoop, calls=%fused_computation.150 | loop fusion | flops 13107200 | bytes 3179520 | tf_op jit(solution)/shard_map/convert.7
  217.5 0.8 fusion.6
  218.4 9.2 %fusion.60 = (bf16[64,4096]{1,0:T(8,128)(2,1)S(1)}, bf16[64,4096]{1,0:T(8,128)(2,1)S(1)}, bf16[64,4096]{1,0:T(8,128)(2,1)S(1)}, bf16[64,4096]{1,0:T(8,128)(2,1)S(1)}) fusion(s32[4096]{0:T(1024)S(1)} %get-tuple-element.68, s32[64]{0:T(128)S(1)} %get-tuple-element.59, s32[4096]{0:T(1024)S(1)} %get-tuple-element.67, s32[64]{0:T(128)S(1)} %get-tuple-element.74, ...), kind=kLoop, calls=%fused_computation.146 | loop fusion | flops 13107200 | bytes 3179520 | tf_op jit(solution)/shard_map/convert.9
  227.6 0.8 fusion.5
  228.5 0.8 fusion.4
  229.4 0.8 fusion.3
  230.3 0.8 fusion.2
  231.2 0.9 fusion.1
  232.1 0.2 fusion.96
  232.3 148.6 %pmax.7 = f32[64]{0:T(128)S(1)} all-reduce(f32[64]{0:T(128)S(1)} %fusion.96), channel_id=1, replica_groups=mesh['orient'=64,'dom'=4] {'orient'}, use_global_device_ids=true, to_apply=%region_1.2 | all-reduce | flops 64 | bytes 512 | tf_op jit(solution)/shard_map/pmax | solution.py:82
  380.9 0.3 exponential_reduce_fusion
  381.2 150.6 %psum.7 = f32[64]{0:T(128)S(1)} all-reduce(f32[64]{0:T(128)S(1)} %exponential_reduce_fusion), channel_id=1, replica_groups=mesh['orient'=64,'dom'=4] {'orient'}, use_global_device_ids=true, to_apply=%region_3.4 | all-reduce | flops 64 | bytes 512 | tf_op jit(solution)/shard_map/psum | solution.py:83
  531.8 0.2 fusion.129
  532.0 0.7 fusion.77
  532.7 0.3 copy-done.14
  533.0 0.2 copy-done.16
  533.2 0.7 convolution_add_fusion.7
  533.9 0.3 copy-done.22
  534.2 0.2 copy-done.24
  534.4 0.7 convolution_add_fusion.6
  535.1 0.3 copy-done.26
  535.4 0.2 copy-done.28
  535.6 0.7 convolution_add_fusion.5
  536.3 0.3 copy-done.34
  536.6 0.2 copy-done.36
  536.8 0.7 convolution_add_fusion.4
  537.5 0.3 copy-done.30
  537.8 0.2 copy-done.32
  538.0 0.7 convolution_add_fusion.3
  538.7 0.3 copy-done.18
  539.0 0.2 copy-done.20
  539.2 0.7 convolution_add_fusion.2
  539.9 0.3 copy-done.6
  540.2 0.2 copy-done.8
  540.4 0.7 convolution_add_fusion.1
  541.1 0.7 convolution_add_fusion
  541.8 0.3 copy.51
  542.1 0.5 convolution_bitcast_fusion
  542.6 2.1 fusion
  544.7 0.6 dynamic_slice.3
  545.3 114.5 %reduce-scatter.2.cloned.1.call-done = bf16[128,3,1024]{2,0,1:T(8,128)(2,1)} async-done(((bf16[128,3,4096]{2,0,1:T(8,128)(2,1)}), bf16[128,3,1024]{2,0,1:T(8,128)(2,1)}) %reduce-scatter.2.cloned.1.call-update) | async-done | bytes 786448 | tf_op jit(solution)/shard_map/reduce_scatter | solution.py:99
  659.8 1.2 slice.195
  661.0 1.8 copy.36
  662.8 0.2 convert_element_type.139
  663.0 0.8 slice_bitcast_fusion
  (76 shorter events, 0.5 us)
Async XLA Ops:
  7.2 164.0 %copy-start = (f32[64,4096]{1,0:T(8,128)S(1)}, f32[64,4096]{1,0:T(8,128)}, u32[]{:S(2)}) copy-start(f32[64,4096]{1,0:T(8,128)} %param.15) | copy-start | bytes 3145732
  7.2 173.2 %all-gather.3.cloned.1.call-start = ((), (), s32[]{:S(2)}) async-start(), calls=%async_computation.1 | async-start | bytes 1064960 | tf_op jit(solution)/shard_map/all_gather | solution.py:53
  7.9 651.9 %reduce-scatter.2.cloned.1.call-start = ((), (), s32[]{:S(2)}) async-start(), calls=%async_computation.2 | async-start | bytes 3932160 | tf_op jit(solution)/shard_map/reduce_scatter | solution.py:99
  171.2 0.9 copy-start.37
  171.2 1.6 copy-start.2
  180.4 6.8 %copy-start.4 = (bf16[16,8,2,4096]{3,1,2,0:T(8,128)(2,1)S(1)}, bf16[16,8,2,4096]{3,1,2,0:T(8,128)(2,1)}, u32[]{:S(2)}) copy-start(bf16[16,8,2,4096]{3,1,2,0:T(8,128)(2,1)} %copy.40) | copy-start | bytes 6291460
  187.1 0.9 copy-start.9
  187.1 9.9 %copy-start.11 = (bf16[64,4096]{1,0:T(8,128)(2,1)}, bf16[64,4096]{1,0:T(8,128)(2,1)S(1)}, u32[]{:S(2)}) copy-start(bf16[64,4096]{1,0:T(8,128)(2,1)S(1)} %get-tuple-element.36) | copy-start | bytes 1572868
  197.1 0.9 copy-start.13
  197.1 10.4 %copy-start.15 = (bf16[64,4096]{1,0:T(8,128)(2,1)}, bf16[64,4096]{1,0:T(8,128)(2,1)S(1)}, u32[]{:S(2)}) copy-start(bf16[64,4096]{1,0:T(8,128)(2,1)S(1)} %get-tuple-element.38) | copy-start | bytes 1572868
  207.5 0.9 copy-start.21
  207.5 9.9 %copy-start.23 = (bf16[64,4096]{1,0:T(8,128)(2,1)}, bf16[64,4096]{1,0:T(8,128)(2,1)S(1)}, u32[]{:S(2)}) copy-start(bf16[64,4096]{1,0:T(8,128)(2,1)S(1)} %get-tuple-element.40) | copy-start | bytes 1572868
  207.5 22.7 %copy-start.5 = (bf16[64,4096]{1,0:T(8,128)(2,1)}, bf16[64,4096]{1,0:T(8,128)(2,1)S(1)}, u32[]{:S(2)}) copy-start(bf16[64,4096]{1,0:T(8,128)(2,1)S(1)} %get-tuple-element.21) | copy-start | bytes 1572868
  207.6 22.7 %copy-start.7 = (bf16[64,4096]{1,0:T(8,128)(2,1)}, bf16[64,4096]{1,0:T(8,128)(2,1)S(1)}, u32[]{:S(2)}) copy-start(bf16[64,4096]{1,0:T(8,128)(2,1)S(1)} %get-tuple-element.22) | copy-start | bytes 1572868
  217.5 10.1 %copy-start.25 = (bf16[64,4096]{1,0:T(8,128)(2,1)}, bf16[64,4096]{1,0:T(8,128)(2,1)S(1)}, u32[]{:S(2)}) copy-start(bf16[64,4096]{1,0:T(8,128)(2,1)S(1)} %get-tuple-element.41) | copy-start | bytes 1572868
  217.5 10.1 %copy-start.27 = (bf16[64,4096]{1,0:T(8,128)(2,1)}, bf16[64,4096]{1,0:T(8,128)(2,1)S(1)}, u32[]{:S(2)}) copy-start(bf16[64,4096]{1,0:T(8,128)(2,1)S(1)} %get-tuple-element.42) | copy-start | bytes 1572868
  217.5 11.9 %copy-start.17 = (bf16[64,4096]{1,0:T(8,128)(2,1)}, bf16[64,4096]{1,0:T(8,128)(2,1)S(1)}, u32[]{:S(2)}) copy-start(bf16[64,4096]{1,0:T(8,128)(2,1)S(1)} %get-tuple-element.23) | copy-start | bytes 1572868
  217.5 11.9 %copy-start.19 = (bf16[64,4096]{1,0:T(8,128)(2,1)}, bf16[64,4096]{1,0:T(8,128)(2,1)S(1)}, u32[]{:S(2)}) copy-start(bf16[64,4096]{1,0:T(8,128)(2,1)S(1)} %get-tuple-element.24) | copy-start | bytes 1572868
  227.6 1.7 copy-start.29
  227.6 1.7 copy-start.31
  227.6 1.7 copy-start.33
  227.6 1.7 copy-start.35
  231.1 0.9 copy-start.38
  231.1 300.8 %copy-start.10 = (bf16[64,4096]{1,0:T(8,128)(2,1)S(1)}, bf16[64,4096]{1,0:T(8,128)(2,1)}, u32[]{:S(2)}) copy-start(bf16[64,4096]{1,0:T(8,128)(2,1)} %copy-done.9) | copy-start | bytes 1572868
  231.1 300.8 %copy-start.12 = (bf16[64,4096]{1,0:T(8,128)(2,1)S(1)}, bf16[64,4096]{1,0:T(8,128)(2,1)}, u32[]{:S(2)}) copy-start(bf16[64,4096]{1,0:T(8,128)(2,1)} %copy-done.11) | copy-start | bytes 1572868
  532.0 1.0 copy-start.14
  532.0 1.2 copy-start.16
  533.2 1.0 copy-start.22
  533.2 1.2 copy-start.24
  534.4 1.0 copy-start.26
  534.4 1.2 copy-start.28
  535.6 1.0 copy-start.34
  535.6 1.2 copy-start.36
  536.8 1.0 copy-start.30
  536.8 1.2 copy-start.32
  538.0 1.0 copy-start.18
  538.0 1.2 copy-start.20
  539.2 1.0 copy-start.6
  539.2 1.2 copy-start.8
  659.8 3.0 copy-start.3
  661.0 2.8 copy-start.1
Sparse Core Ops, SparseCore 0:
  11.5 113.1 all-gather.2
  544.8 114.8 reduce-scatter.1
where the time goes:
time: 674 us; the launch traced here: 671 us
  blocking collectives  456 us (68%)
  waiting for transfers between devices  115 us (17%)
  other arithmetic  47.3 us (7%)
  matrix products  18.3 us (3%)
  local copies, waits for them, and re-layouts  18.1 us (3%)
  between operations  16.2 us (2%)
    all_gather x1, blocking collectives, on_device(): lax.all_gather(meta, 'orient', axis=0, tiled=True)  157 us
    psum x1, blocking collectives, on_device(): lax.psum(jnp.sum(jnp.exp(score - top[None, :, None]), axis=(0, 2)), 'orie...  151 us
    pmax x1, blocking collectives, on_device(): top = lax.pmax(local_top, 'orient')  149 us
    reduce_scatter x1, waiting for transfers between devices, on_device(): lax.psum_scatter(stacked.astype(jnp.bfloat16), 'dom', scatter_dimension=2...  114 us
    another operation x6, other arithmetic  42.2 us
  transfers between devices with their start and end apart: 2, of which 1 were waited for; matrix products, arithmetic and copies ran while one was open for 2% of the time, Pallas kernels for 0%

commit v1 on v0

--- a/solution.py
+++ b/solution.py
@@ -80,7 +80,9 @@
     score = cross - 0.5 * self_term[None, :, :] + prior.T[:, :, None] + log_prior[None, None, :]
     local_top = jnp.max(score, axis=(0, 2))
     top = lax.pmax(local_top, "orient")
-    mass = lax.psum(jnp.sum(jnp.exp(score - top[None, :, None]), axis=(0, 2)), "orient")
+    mass = jnp.sum(
+        lax.all_gather(jnp.sum(jnp.exp(score - top[None, :, None]), axis=(0, 2)), "orient"), axis=0
+    )
     evidence = top + jnp.log(mass)
     post = jnp.exp(score - evidence[None, :, None]).astype(jnp.bfloat16)
     post_sum = jnp.sum(post.astype(jnp.float32), axis=0).astype(jnp.bfloat16)

time: 674 us -> 850 us (1.26)
  blocking collectives: 456 us -> 603 us
  waiting for transfers between devices: 115 us -> 143 us
    unnamed x0 -> x1, blocking collectives: none -> 297 us
    psum x1 -> x0, blocking collectives: 151 us -> none  [on_device(): lax.psum(jnp.sum(jnp.exp(score - top[None, :, None]), axis=(0, 2)), 'orie...]
    reduce_scatter x1, waiting for transfers between devices: 114 us -> 142 us  [on_device(): lax.psum_scatter(stacked.astype(jnp.bfloat16), 'dom', scatter_dimension=2...]
where the time goes in v1:
time: 850 us; the launch traced here: 847 us
  blocking collectives  603 us (71%)
  waiting for transfers between devices  143 us (17%)
  other arithmetic  47.3 us (6%)
  local copies, waits for them, and re-layouts  19 us (2%)
  matrix products  18.3 us (2%)
  between operations  16.9 us (2%)
    unnamed x1, blocking collectives  297 us
    all_gather x1, blocking collectives, on_device(): lax.all_gather(meta, 'orient', axis=0, tiled=True)  157 us
    pmax x1, blocking collectives, on_device(): top = lax.pmax(local_top, 'orient')  149 us
    reduce_scatter x1, waiting for transfers between devices, on_device(): lax.psum_scatter(stacked.astype(jnp.bfloat16), 'dom', scatter_dimension=2...  142 us
    another operation x6, other arithmetic  42.2 us
  transfers between devices with their start and end apart: 2, of which 1 were waited for; matrix products, arithmetic and copies ran while one was open for 2% of the time, Pallas kernels for 0%

profile of v1, /device:TPU:1, one launch (start us, length us, event | category | flops | bytes accessed | tf_op | source)
XLA Modules:
  0.0 846.9 jit_solution(13477488853204897887)
XLA Ops:
  7.2 0.7 all-gather.4.cloned.1.call-update
  8.0 0.7 convert.69
  8.6 0.1 copy.38
  10.2 156.5 %all-gather.1 = bf16[64,1,20]{2,1,0:T(2,128)(2,1)S(1)} all-gather(bf16[1,1,20]{2,1,0:T(2,128)(2,1)S(1)} %maximum_bitcast_fusion), channel_id=1, replica_groups=mesh['orient'=64,'dom'=4] {'orient'}, dimensions={0}, use_global_device_ids=true | all-gather | bytes 2600 | tf_op jit(solution)/shard_map/all_gather | solution.py:54
  167.0 4.2 copy.47
  171.2 0.6 dynamic-slice
  172.5 0.6 fusion.97
  173.1 0.6 multiply_convert_fusion.1
  173.8 0.3 copy-done.2
  174.0 5.1 fusion.130
  179.1 2.4 convolution_multiply_fusion.1
  181.6 2.0 multiply_convert_fusion
  183.6 4.7 fusion.40
  188.3 0.9 fusion.9
  189.2 9.0 %fusion.72 = (bf16[64,4096]{1,0:T(8,128)(2,1)S(1)}, bf16[64,4096]{1,0:T(8,128)(2,1)S(1)}, bf16[64,4096]{1,0:T(8,128)(2,1)S(1)}, bf16[64,4096]{1,0:T(8,128)(2,1)S(1)}) fusion(s32[4096]{0:T(1024)S(1)} %get-tuple-element.71, s32[64]{0:T(128)S(1)} %get-tuple-element.59, s32[4096]{0:T(1024)S(1)} %get-tuple-element.70, s32[64]{0:T(128)S(1)} %get-tuple-element.80, ...), kind=kLoop, calls=%fused_computation.158 | loop fusion | flops 13107200 | bytes 3179520 | tf_op jit(solution)/shard_map/convert.3
  198.3 0.8 fusion.8
  199.1 9.6 %fusion.68 = (bf16[64,4096]{1,0:T(8,128)(2,1)S(1)}, bf16[64,4096]{1,0:T(8,128)(2,1)S(1)}, bf16[64,4096]{1,0:T(8,128)(2,1)S(1)}, bf16[64,4096]{1,0:T(8,128)(2,1)S(1)}) fusion(s32[4096]{0:T(1024)S(1)} %get-tuple-element.71, s32[64]{0:T(128)S(1)} %get-tuple-element.60, s32[4096]{0:T(1024)S(1)} %get-tuple-element.70, s32[64]{0:T(128)S(1)} %get-tuple-element.79, ...), kind=kLoop, calls=%fused_computation.154 | loop fusion | flops 13107200 | bytes 3179520 | tf_op jit(solution)/shard_map/convert.5
  208.7 0.8 fusion.7
  209.6 9.0 %fusion.64 = (bf16[64,4096]{1,0:T(8,128)(2,1)S(1)}, bf16[64,4096]{1,0:T(8,128)(2,1)S(1)}, bf16[64,4096]{1,0:T(8,128)(2,1)S(1)}, bf16[64,4096]{1,0:T(8,128)(2,1)S(1)}) fusion(s32[4096]{0:T(1024)S(1)} %get-tuple-element.71, s32[64]{0:T(128)S(1)} %get-tuple-element.61, s32[4096]{0:T(1024)S(1)} %get-tuple-element.70, s32[64]{0:T(128)S(1)} %get-tuple-element.78, ...), kind=kLoop, calls=%fused_computation.150 | loop fusion | flops 13107200 | bytes 3179520 | tf_op jit(solution)/shard_map/convert.7
  218.7 0.8 fusion.6
  219.6 9.2 %fusion.60 = (bf16[64,4096]{1,0:T(8,128)(2,1)S(1)}, bf16[64,4096]{1,0:T(8,128)(2,1)S(1)}, bf16[64,4096]{1,0:T(8,128)(2,1)S(1)}, bf16[64,4096]{1,0:T(8,128)(2,1)S(1)}) fusion(s32[4096]{0:T(1024)S(1)} %get-tuple-element.71, s32[64]{0:T(128)S(1)} %get-tuple-element.62, s32[4096]{0:T(1024)S(1)} %get-tuple-element.70, s32[64]{0:T(128)S(1)} %get-tuple-element.77, ...), kind=kLoop, calls=%fused_computation.146 | loop fusion | flops 13107200 | bytes 3179520 | tf_op jit(solution)/shard_map/convert.9
  228.8 0.8 fusion.5
  229.7 0.8 fusion.4
  230.6 0.8 fusion.3
  231.5 0.8 fusion.2
  232.3 0.9 fusion.1
  233.2 0.2 fusion.96
  233.5 148.6 %pmax.7 = f32[64]{0:T(128)S(1)} all-reduce(f32[64]{0:T(128)S(1)} %fusion.96), channel_id=1, replica_groups=mesh['orient'=64,'dom'=4] {'orient'}, use_global_device_ids=true, to_apply=%region_1.2 | all-reduce | flops 64 | bytes 512 | tf_op jit(solution)/shard_map/pmax | solution.py:82
  382.1 0.3 exponential_reduce_fusion
  382.4 0.3 dynamic-update-slice
  382.7 297.4 %all-reduce = f32[4096]{0:T(1024)S(1)} all-reduce(f32[4096]{0:T(1024)S(1)} %dynamic-update-slice), channel_id=2, replica_groups=mesh['orient'=64,'dom'=4] {'orient'}, use_global_device_ids=true, to_apply=%add | all-reduce | flops 4096 | bytes 32768
  680.2 0.2 fusion.129
  680.4 0.7 fusion.77
  681.2 0.3 copy-done.14
  681.5 0.2 copy-done.16
  681.6 0.7 convolution_add_fusion.7
  682.4 0.3 copy-done.22
  682.7 0.2 copy-done.24
  682.8 0.7 convolution_add_fusion.6
  683.6 0.3 copy-done.26
  683.9 0.2 copy-done.28
  684.0 0.7 convolution_add_fusion.5
  684.8 0.3 copy-done.34
  685.1 0.2 copy-done.36
  685.2 0.7 convolution_add_fusion.4
  686.0 0.3 copy-done.30
  686.3 0.2 copy-done.32
  686.4 0.7 convolution_add_fusion.3
  687.2 0.3 copy-done.18
  687.5 0.2 copy-done.20
  687.6 0.7 convolution_add_fusion.2
  688.4 0.3 copy-done.6
  688.7 0.2 copy-done.8
  688.8 0.7 convolution_add_fusion.1
  689.6 0.7 convolution_add_fusion
  690.3 0.3 copy.58
  690.6 0.5 convolution_bitcast_fusion
  691.1 2.1 fusion
  693.2 0.6 dynamic_slice.3
  693.8 142.0 %reduce-scatter.2.cloned.1.call-done = bf16[128,3,1024]{2,0,1:T(8,128)(2,1)} async-done(((bf16[128,3,4096]{2,0,1:T(8,128)(2,1)}), bf16[128,3,1024]{2,0,1:T(8,128)(2,1)}) %reduce-scatter.2.cloned.1.call-update) | async-done | bytes 786448 | tf_op jit(solution)/shard_map/reduce_scatter | solution.py:101
  835.8 1.2 slice.195
  837.0 1.8 copy.43
  838.8 0.2 convert_element_type.139
  839.0 0.8 slice_bitcast_fusion
  (83 shorter events, 0.7 us)
Async XLA Ops:
  7.2 165.3 %copy-start = (f32[64,4096]{1,0:T(8,128)S(1)}, f32[64,4096]{1,0:T(8,128)}, u32[]{:S(2)}) copy-start(f32[64,4096]{1,0:T(8,128)} %param.15) | copy-start | bytes 3145732
  7.2 174.4 %all-gather.4.cloned.1.call-start = ((), (), s32[]{:S(2)}) async-start(), calls=%async_computation.1 | async-start | bytes 1064960 | tf_op jit(solution)/shard_map/all_gather | solution.py:53
  7.9 827.9 %reduce-scatter.2.cloned.1.call-start = ((), (), s32[]{:S(2)}) async-start(), calls=%async_computation.2 | async-start | bytes 3932160 | tf_op jit(solution)/shard_map/reduce_scatter | solution.py:101
  166.9 4.2 copy-start.39
  171.2 1.9 copy-start.37
  172.4 1.6 copy-start.2
  181.6 6.8 copy-start.4
  188.3 0.9 copy-start.9
  188.3 9.9 %copy-start.11 = (bf16[64,4096]{1,0:T(8,128)(2,1)}, bf16[64,4096]{1,0:T(8,128)(2,1)S(1)}, u32[]{:S(2)}) copy-start(bf16[64,4096]{1,0:T(8,128)(2,1)S(1)} %get-tuple-element.39) | copy-start | bytes 1572868
  198.2 0.9 copy-start.13
  198.3 10.4 %copy-start.15 = (bf16[64,4096]{1,0:T(8,128)(2,1)}, bf16[64,4096]{1,0:T(8,128)(2,1)S(1)}, u32[]{:S(2)}) copy-start(bf16[64,4096]{1,0:T(8,128)(2,1)S(1)} %get-tuple-element.41) | copy-start | bytes 1572868
  208.7 0.9 copy-start.21
  208.7 9.9 %copy-start.23 = (bf16[64,4096]{1,0:T(8,128)(2,1)}, bf16[64,4096]{1,0:T(8,128)(2,1)S(1)}, u32[]{:S(2)}) copy-start(bf16[64,4096]{1,0:T(8,128)(2,1)S(1)} %get-tuple-element.43) | copy-start | bytes 1572868
  208.7 22.7 %copy-start.5 = (bf16[64,4096]{1,0:T(8,128)(2,1)}, bf16[64,4096]{1,0:T(8,128)(2,1)S(1)}, u32[]{:S(2)}) copy-start(bf16[64,4096]{1,0:T(8,128)(2,1)S(1)} %get-tuple-element.24) | copy-start | bytes 1572868
  208.7 22.7 %copy-start.7 = (bf16[64,4096]{1,0:T(8,128)(2,1)}, bf16[64,4096]{1,0:T(8,128)(2,1)S(1)}, u32[]{:S(2)}) copy-start(bf16[64,4096]{1,0:T(8,128)(2,1)S(1)} %get-tuple-element.25) | copy-start | bytes 1572868
  218.7 10.1 %copy-start.25 = (bf16[64,4096]{1,0:T(8,128)(2,1)}, bf16[64,4096]{1,0:T(8,128)(2,1)S(1)}, u32[]{:S(2)}) copy-start(bf16[64,4096]{1,0:T(8,128)(2,1)S(1)} %get-tuple-element.44) | copy-start | bytes 1572868
  218.7 10.1 %copy-start.27 = (bf16[64,4096]{1,0:T(8,128)(2,1)}, bf16[64,4096]{1,0:T(8,128)(2,1)S(1)}, u32[]{:S(2)}) copy-start(bf16[64,4096]{1,0:T(8,128)(2,1)S(1)} %get-tuple-element.45) | copy-start | bytes 1572868
  218.7 11.9 %copy-start.17 = (bf16[64,4096]{1,0:T(8,128)(2,1)}, bf16[64,4096]{1,0:T(8,128)(2,1)S(1)}, u32[]{:S(2)}) copy-start(bf16[64,4096]{1,0:T(8,128)(2,1)S(1)} %get-tuple-element.26) | copy-start | bytes 1572868
  218.7 11.9 %copy-start.19 = (bf16[64,4096]{1,0:T(8,128)(2,1)}, bf16[64,4096]{1,0:T(8,128)(2,1)S(1)}, u32[]{:S(2)}) copy-start(bf16[64,4096]{1,0:T(8,128)(2,1)S(1)} %get-tuple-element.27) | copy-start | bytes 1572868
  228.8 1.7 copy-start.29
  228.8 1.7 copy-start.31
  228.8 1.7 copy-start.33
  228.8 1.7 copy-start.35
  232.3 0.9 copy-start.38
  232.3 448.1 %copy-start.10 = (bf16[64,4096]{1,0:T(8,128)(2,1)S(1)}, bf16[64,4096]{1,0:T(8,128)(2,1)}, u32[]{:S(2)}) copy-start(bf16[64,4096]{1,0:T(8,128)(2,1)} %copy-done.9) | copy-start | bytes 1572868
  232.3 448.1 %copy-start.12 = (bf16[64,4096]{1,0:T(8,128)(2,1)S(1)}, bf16[64,4096]{1,0:T(8,128)(2,1)}, u32[]{:S(2)}) copy-start(bf16[64,4096]{1,0:T(8,128)(2,1)} %copy-done.11) | copy-start | bytes 1572868
  680.4 1.0 copy-start.14
  680.4 1.2 copy-start.16
  681.6 1.0 copy-start.22
  681.6 1.2 copy-start.24
  682.8 1.0 copy-start.26
  682.8 1.2 copy-start.28
  684.0 1.0 copy-start.34
  684.0 1.2 copy-start.36
  685.2 1.0 copy-start.30
  685.2 1.2 copy-start.32
  686.4 1.0 copy-start.18
  686.4 1.2 copy-start.20
  687.6 1.0 copy-start.6
  687.6 1.2 copy-start.8
  835.8 3.0 copy-start.3
  837.0 2.8 copy-start.1
Sparse Core Ops, SparseCore 0:
  11.5 113.1 all-gather.3
  693.3 142.4 reduce-scatter.1
